TPU v7x, 32 devices: a whole 2x2x4 slice. The times are simulated.
32 devices in a mesh: row: 8 (over z, core), col: 4 (over y, x).
Axes of the slice: x: 2, y: 2, z: 4, core: 2. Of those that a mesh axis runs over, the one named last changes fastest.
Arguments:
- object_field: float32 [2, 2048, 1024], P(None, 'row', 'col'), may hold values from -1.8 to 1.8
- probe: float32 [2, 256, 256], replicated, may hold values from -0.4 to 0.4
- coeffs: float32 [3, 256, 256], replicated, may hold values from 0.5 to 1.5
- patterns: float32 [8, 4, 4, 256, 256], P('row', 'col'), may hold values from 0 to 1
- offsets: int32 [8, 4, 4, 2], P('row', 'col'), may hold values from 0 to 255
Outputs:
- object_out: float32 [2, 2048, 1024], P(None, 'row', 'col')
- coeffs_out: float32 [3, 256, 256], replicated
All inputs are finite; a program needn't handle non-finite values.
Results may differ from a plain program's by a relative error of at most 0.0003.
Values sent between devices are 32-bit elements; how exact they have to be, the bound alone decides.
A program may use at most 64 MiB of HBM per device.

v0:
```python
import functools

import jax
import jax.numpy as jnp
import ml_dtypes
import numpy as np
from jax import lax
from jax.experimental import pallas as pl
from jax.experimental.pallas import tpu as pltpu
from jax.sharding import PartitionSpec as P

ITERS = 2


STEP_RATE = 0.2
RIDGE = 1.0
EPSILON = 1e-06


def passed_along(block, axis, distance):
    devices = range(lax.axis_size(axis))
    route = [(i - distance, i) for i in devices if i - distance in devices]
    return lax.ppermute(block, axis, route)


def padded(block, sides, width):
    for axis, dim in sides:
        count = lax.axis_size(axis)
        forward = [(i, i + 1) for i in range(count - 1)]
        backward = [(target, source) for source, target in forward]
        low = lax.ppermute(
            lax.slice_in_dim(block, block.shape[dim] - width, None, axis=dim), axis, forward
        )
        high = lax.ppermute(lax.slice_in_dim(block, 0, width, axis=dim), axis, backward)
        block = jnp.concatenate([low, block, high], axis=dim)
    return block


def dft_stacks(order):
    index = np.arange(order)
    angle = -2.0 * np.pi / order * (index[:, None] * index[None, :] % order)
    real, imag = np.cos(angle) / np.sqrt(order), np.sin(angle) / np.sqrt(order)
    left = np.block([[real, -imag], [imag, real]]).astype(np.float32)
    stacks = []
    for full in (left, left.T):
        high = full.astype(ml_dtypes.bfloat16)
        low = (full - high.astype(np.float32)).astype(ml_dtypes.bfloat16)
        stacks += [high, low]
    return [jnp.asarray(stack) for stack in stacks]


def dot(left, right):
    return jnp.dot(left, right, preferred_element_type=jnp.float32)


def split(full):
    high = full.astype(jnp.bfloat16)
    return high, (full - high.astype(jnp.float32)).astype(jnp.bfloat16)


def transform(real, imag, left_high, left_low, right_high, right_low):
    width = real.shape[0]
    high, low = split(jnp.concatenate([real, imag], axis=0))
    rows = dot(left_high, high) + dot(left_high, low) + dot(left_low, high)
    high, low = split(jnp.concatenate([rows[:width], rows[width:]], axis=1))
    cols = dot(high, right_high) + dot(low, right_high) + dot(high, right_low)
    return cols[:, :width], cols[:, width:]


def visit_kernel(offs, ext, probe, coeffs, pats, ah, al, bh, bl, grad, stats, shifted):
    width = probe.shape[1]
    size = ext.shape[1]
    tile = size - width
    grad[...] = jnp.zeros_like(grad)
    stats[...] = jnp.zeros_like(stats)
    shifted[...] = jnp.zeros_like(shifted)

    def visit(p, carry):
        oy, ox = offs[p, 0], offs[p, 1]
        odd = lax.rem(oy, 8)
        even = pl.multiple_of(oy - odd, 8)
        window = []
        for part in (0, 1):
            rows = pltpu.roll(ext[part, pl.ds(even, width + 8), :], lax.rem(size - ox, size), axis=1)
            rows = pltpu.roll(rows[:, :width], lax.rem(width + 8 - odd, width + 8), axis=0)
            window.append(rows[:width])
        pr, pi = probe[0], probe[1]
        wr, wi = transform(
            pr * window[0] - pi * window[1],
            pr * window[1] + pi * window[0],
            ah[...], al[...], bh[...], bl[...],
        )
        inten = wr * wr + wi * wi
        lin, quad, cubic = coeffs[0], coeffs[1], coeffs[2]
        error = inten * (lin + inten * (quad + inten * cubic)) - pats[p]
        weight = 2.0 * error * (lin + inten * (2.0 * quad + 3.0 * cubic * inten))
        squared = inten * inten
        cubed = squared * inten
        stats[0] += error * inten
        stats[1] += error * squared
        stats[2] += error * cubed
        stats[3] += squared
        stats[4] += squared * squared
        stats[5] += cubed * cubed
        br, bi = transform(weight * wr, weight * wi, bh[...], bl[...], ah[...], al[...])
        below = jnp.zeros((8, width), jnp.float32)
        beside = jnp.zeros((width + 8, tile), jnp.float32)
        for part, g in ((0, pr * br + pi * bi), (1, pr * bi - pi * br)):
            g = pltpu.roll(jnp.concatenate([g, below], axis=0), odd, axis=0)
            g = pltpu.roll(jnp.concatenate([g, beside], axis=1), ox, axis=1)
            shifted[part, tile : tile + width + 8, :] = g
            grad[part] += shifted[part, pl.ds(pl.multiple_of(tile - even, 8), size), :]
        return carry

    lax.fori_loop(0, pats.shape[0], visit, 0)


def visit_windows(offs, ext, probe, coeffs, pats, stacks):
    width = probe.shape[1]
    size = ext.shape[1]
    vmem = pl.BlockSpec(memory_space=pltpu.VMEM)
    return pl.pallas_call(
        visit_kernel,
        out_shape=(
            jax.ShapeDtypeStruct(ext.shape, jnp.float32),
            jax.ShapeDtypeStruct((6, width, width), jnp.float32),
        ),
        in_specs=[pl.BlockSpec(memory_space=pltpu.SMEM)] + [vmem] * 8,
        out_specs=(vmem, vmem),
        scratch_shapes=[pltpu.VMEM((2, 2 * (size - width) + width, size), jnp.float32)],
        compiler_params=pltpu.CompilerParams(vmem_limit_bytes=40 * 1024 * 1024),
        name="visit_windows",
    )(offs, ext, probe, coeffs, pats, *stacks)


def fold_rows(grad_ext, half):
    received = []
    for toward, border in ((-1, grad_ext[:, :half, :]), (1, grad_ext[:, -half:, :])):
        received.append(passed_along(border, "row", toward))
    middle = grad_ext[:, half:-half, :]
    return middle.at[:, -half:, :].add(received[0]).at[:, :half, :].add(received[1])


def fold_cols(grad_mid, half):
    received = []
    for toward, border in ((-1, grad_mid[:, :, :half]), (1, grad_mid[:, :, -half:])):
        received.append(passed_along(border, "col", toward))
    middle = grad_mid[:, :, half:-half]
    return middle.at[:, :, -half:].add(received[0]).at[:, :, :half].add(received[1])


def local(object_field, probe, coeffs, patterns, offsets):
    width = probe.shape[1]
    half = width // 2
    tile = object_field.shape[1]
    stacks = dft_stacks(width)
    flat_pats = patterns.reshape(-1, width, width)
    flat_offs = offsets.reshape(-1, 2)
    devices = lax.axis_size("row") * lax.axis_size("col")
    total = 2.0 * tile * tile * devices
    for turn in range(ITERS):
        extended = padded(object_field, (("row", 1), ("col", 2)), half)
        grad_ext, stats = visit_windows(flat_offs, extended, probe, coeffs, flat_pats, stacks)
        stats = lax.psum(stats, ("row", "col"))
        new_coeffs = coeffs - stats[:3] / (stats[3:] + RIDGE)
        grad = fold_cols(fold_rows(grad_ext, half), half)
        sumsq = lax.psum(jnp.sum(grad * grad), ("row", "col"))
        object_field = object_field - STEP_RATE * grad / jnp.sqrt(sumsq / total + EPSILON)
        coeffs = new_coeffs
    return (object_field, coeffs)


def solution(mesh):
    placed = (
        P(None, "row", "col"),
        P(),
        P(),
        P("row", "col", None, None, None),
        P("row", "col", None, None),
    )
    return jax.shard_map(
        local, mesh=mesh, in_specs=placed, out_specs=(P(None, "row", "col"), P()), check_vma=False
    )
```

profile of v0, /device:TPU:0, one launch (start us, length us, event | category | flops | bytes accessed | tf_op | source)
XLA Modules:
  0.0 466.1 jit_solution(12693029741612597980)
XLA Ops:
  7.2 0.0 all-reduce.3.cloned.1.call-start
  7.2 1.1 fusion.17
  8.3 2.4 collective-permute-start
  10.7 1.3 collective-permute-start.1
  12.0 1.1 constant_dynamic-update-slice_fusion.1
  13.1 3.2 collective-permute-done.1
  16.3 0.9 fusion.15
  17.2 4.2 collective-permute-start.2
  21.4 1.3 collective-permute-start.3
  22.7 0.1 copy.11.offs
  22.8 6.5 %collective-permute-done.2 = f32[2,512,128]{2,1,0:T(8,128)} collective-permute-done((f32[2,512,128]{2,1,0:T(8,128)}, f32[2,512,128]{2,1,0:T(8,128)}, u32[]{:S(2)}, u32[]{:S(2)}) %collective-permute-start.2) | collective-permute-done | bytes 524320 | tf_op jit(solution)/shard_map/ppermute | solution.py:31
  29.3 13.2 %collective-permute-done.3 = f32[2,512,128]{2,1,0:T(8,128)} collective-permute-done((f32[2,512,128]{2,1,0:T(8,128)S(1)}, f32[2,512,128]{2,1,0:T(8,128)}, u32[]{:S(2)}, u32[]{:S(2)}) %collective-permute-start.3) | collective-permute-done | bytes 524320 | tf_op jit(solution)/shard_map/ppermute | solution.py:34
  42.5 1.7 pad_maximum_fusion.ext
  44.3 20.2 %visit_windows.2 = (f32[2,512,512]{2,1,0:T(8,128)S(1)}, f32[6,256,256]{2,1,0:T(8,128)S(1)}) custom-call(s32[4,2]{1,0:T(4,128)S(1)} %copy.11.offs, f32[2,512,512]{2,1,0:T(8,128)S(1)} %pad_maximum_fusion.ext, f32[2,256,256]{2,1,0:T(8,128)S(1)} %copy-done.2, f32[3,256,256]{2,1,0:T(8,128)S(1)} %copy-done.1, f32[4,256,256]{2,1,0:T(8,128)S(1)} %bitcast.2, ...), custom_call_target="tpu_custom_call" | custom-call | tf_op jit(solution)/shard_map/visit_windows/pallas_call | solution.py:122
  64.5 0.1 fusion.11
  64.6 1.3 collective-permute-start.4
  65.9 6.2 %collective-permute-start.5 = (f32[2,128,512]{2,1,0:T(8,128)S(1)}, f32[2,128,512]{2,1,0:T(8,128)S(1)}, u32[]{:S(2)}, u32[]{:S(2)}) collective-permute-start(f32[2,128,512]{2,1,0:T(8,128)S(1)} %get-tuple-element.108), channel_id=1, source_target_pairs={{0,4},{4,8},{8,12},{12,16},{16,20},{20,24},{24,28},{1,5},{5,9},{9,... | collective-permute-start | bytes 1572872 | tf_op jit(solution)/shard_map/ppermute | solution.py:23
  72.2 0.1 slice.272
  72.3 0.1 add_dynamic-update-slice_fusion.1
  72.4 1.3 collective-permute-done.5
  73.7 0.1 fusion.5
  73.9 1.3 collective-permute-start.6
  75.2 4.6 collective-permute-start.7
  79.8 2.4 collective-permute-done.6
  82.1 0.1 fusion.9
  82.2 1.4 collective-permute-done.7
  83.6 0.1 fusion.8
  83.6 0.7 multiply_reduce_fusion.1
  84.4 55.8 %psum.28 = f32[]{:T(128)} all-reduce(f32[]{:T(128)} %multiply_reduce_fusion.1), channel_id=1, replica_groups=mesh['row'=8,'col'=4] {'row','col'}, use_global_device_ids=true, to_apply=%region_1.0 | all-reduce | flops 1 | bytes 8 | tf_op jit(solution)/shard_map/psum | solution.py:167
  140.9 1.1 divide_subtract_fusion.1
  142.0 0.9 fusion.16
  142.9 1.3 collective-permute-start.8
  144.2 1.3 collective-permute-start.9
  145.5 0.0 all-reduce.3.cloned.1.call-update
  145.6 0.0 all-reduce.5.cloned.1.call-start
  145.6 2.4 collective-permute-done.9
  148.0 0.1 pad_maximum_fusion.2
  148.1 1.0 fusion.13
  149.2 5.0 %collective-permute-start.10 = (f32[2,512,128]{2,1,0:T(8,128)}, f32[2,512,128]{2,1,0:T(8,128)}, u32[]{:S(2)}, u32[]{:S(2)}) collective-permute-start(f32[2,512,128]{2,1,0:T(8,128)} %get-tuple-element.112), channel_id=1, source_target_pairs={{0,1},{1,2},{2,3},{4,5},{5,6},{6,7},{8,9},{9,10},{10,11},{12,13},{... | collective-permute-start | bytes 1572872 | tf_op jit(solution)/shard_map/ppermute | solution.py:31
  154.1 1.3 collective-permute-start.11
  155.4 125.3 %all-reduce.3.cloned.1.call-done = f32[6,256,256]{2,1,0:T(8,128)} async-done(((f32[6,256,256]{2,1,0:T(8,128)}), f32[6,256,256]{2,1,0:T(8,128)}) %all-reduce.3.cloned.1.call-update) | async-done | bytes 1572880 | tf_op jit(solution)/shard_map/psum | solution.py:164
  280.7 1.6 fusion.3.coeffs
  282.4 1.5 pad_maximum_fusion.1.ext
  284.0 0.2 copy-done.10
  284.2 21.4 %visit_windows.3 = (f32[2,512,512]{2,1,0:T(8,128)S(1)}, f32[6,256,256]{2,1,0:T(8,128)}) custom-call(s32[4,2]{1,0:T(4,128)S(1)} %copy.11.offs, f32[2,512,512]{2,1,0:T(8,128)S(1)} %pad_maximum_fusion.1.ext, f32[2,256,256]{2,1,0:T(8,128)S(1)} %copy-done.2, f32[3,256,256]{2,1,0:T(8,128)S(1)} %fusion.3.coeffs, f32[4,256,256]{2,1,0:T(8,128)S(1)} %bitcast.3, ...), custom_call_target="tpu_custom_call" | custom-call | tf_op jit(solution)/shard_map/visit_windows/pallas_call | solution.py:122
  305.5 0.1 fusion.10
  305.6 1.3 collective-permute-start.12
  306.9 3.1 collective-permute-start.13
  310.0 0.1 slice.288
  310.1 0.1 add_dynamic-update-slice_fusion
  310.2 1.3 collective-permute-done.13
  311.5 0.1 fusion.4
  311.6 0.8 fusion.12
  312.4 1.3 collective-permute-start.14
  313.7 4.6 collective-permute-start.15
  318.4 2.5 collective-permute-done.14
  320.9 0.1 fusion.7
  321.0 1.5 collective-permute-done.15
  322.5 0.1 fusion.6
  322.5 0.7 multiply_reduce_fusion
  323.3 52.1 %psum.30 = f32[]{:T(128)} all-reduce(f32[]{:T(128)} %multiply_reduce_fusion), channel_id=1, replica_groups=mesh['row'=8,'col'=4] {'row','col'}, use_global_device_ids=true, to_apply=%region_4.0 | all-reduce | flops 1 | bytes 8 | tf_op jit(solution)/shard_map/psum | solution.py:167
  376.0 0.9 divide_subtract_fusion
  376.9 79.9 %all-reduce.5.cloned.1.call-done = f32[6,256,256]{2,1,0:T(8,128)} async-done(((f32[6,256,256]{2,1,0:T(8,128)}), f32[6,256,256]{2,1,0:T(8,128)}) %all-reduce.5.cloned.1.call-update) | async-done | bytes 1572880 | tf_op jit(solution)/shard_map/psum | solution.py:164
  456.8 2.4 fusion.1
  (49 shorter events, 0.3 us)
Async XLA Ops:
  7.2 273.6 %all-reduce.3.cloned.1.call-start = ((), (), s32[]{:S(2)}) async-start(), calls=%async_computation | async-start | bytes 3145728 | tf_op jit(solution)/shard_map/psum | solution.py:164
  8.3 3.7 collective-permute-start
  10.7 12.0 %copy-start.18 = (s32[1,1,4,2]{2,3,1,0:T(2,128)S(1)}, s32[1,1,4,2]{2,3,1,0:T(2,128)}, u32[]{:S(2)}) copy-start(s32[1,1,4,2]{2,3,1,0:T(2,128)} %param.29) | copy-start | bytes 100
  10.7 5.6 %collective-permute-start.1 = (f32[2,128,256]{2,1,0:T(8,128)S(1)}, f32[2,128,256]{2,1,0:T(8,128)S(1)}, u32[]{:S(2)}, u32[]{:S(2)}) collective-permute-start(f32[2,128,256]{2,1,0:T(8,128)S(1)} %get-tuple-element.120), channel_id=1, source_target_pairs={{4,0},{8,4},{12,8},{16,12},{20,16},{24,20},{28,24},{5,1},{9,5},{13... | collective-permute-start | bytes 786440 | tf_op jit(solution)/shard_map/ppermute | solution.py:34
  16.3 6.4 %copy-start.15 = (f32[2,512,256]{2,1,0:T(8,128)}, f32[2,512,256]{2,1,0:T(8,128)S(1)}, u32[]{:S(2)}) copy-start(f32[2,512,256]{2,1,0:T(8,128)S(1)} %constant_dynamic-update-slice_fusion) | copy-start | bytes 3145732
  16.3 28.0 %copy-start.9 = (bf16[512,512]{1,0:T(8,128)(2,1)S(1)}, bf16[512,512]{1,0:T(8,128)(2,1)}, u32[]{:S(2)}) copy-start(bf16[512,512]{1,0:T(8,128)(2,1)} %constant.206.clone.ah) | copy-start | bytes 1572868
  17.2 12.2 %collective-permute-start.2 = (f32[2,512,128]{2,1,0:T(8,128)}, f32[2,512,128]{2,1,0:T(8,128)}, u32[]{:S(2)}, u32[]{:S(2)}) collective-permute-start(f32[2,512,128]{2,1,0:T(8,128)} %get-tuple-element.116), channel_id=1, source_target_pairs={{0,1},{1,2},{2,3},{4,5},{5,6},{6,7},{8,9},{9,10},{10,11},{12,13},{... | collective-permute-start | bytes 1572872 | tf_op jit(solution)/shard_map/ppermute | solution.py:31
  21.4 21.1 %collective-permute-start.3 = (f32[2,512,128]{2,1,0:T(8,128)S(1)}, f32[2,512,128]{2,1,0:T(8,128)}, u32[]{:S(2)}, u32[]{:S(2)}) collective-permute-start(f32[2,512,128]{2,1,0:T(8,128)S(1)} %get-tuple-element.117), channel_id=1, source_target_pairs={{1,0},{2,1},{3,2},{5,4},{6,5},{7,6},{9,8},{10,9},{11,10},{13,12},{... | collective-permute-start | bytes 1572872 | tf_op jit(solution)/shard_map/ppermute | solution.py:34
  22.8 21.5 %copy-start = (f32[1,1,4,256,256]{4,3,2,1,0:T(8,128)S(1)}, f32[1,1,4,256,256]{4,3,2,1,0:T(8,128)}, u32[]{:S(2)}) copy-start(f32[1,1,4,256,256]{4,3,2,1,0:T(8,128)} %param.28) | copy-start | bytes 3145732
  22.8 21.5 %copy-start.1 = (f32[3,256,256]{2,1,0:T(8,128)S(1)}, f32[3,256,256]{2,1,0:T(8,128)}, u32[]{:S(2)}) copy-start(f32[3,256,256]{2,1,0:T(8,128)} %coeffs.1) | copy-start | bytes 2359300
  22.8 21.5 %copy-start.2 = (f32[2,256,256]{2,1,0:T(8,128)S(1)}, f32[2,256,256]{2,1,0:T(8,128)}, u32[]{:S(2)}) copy-start(f32[2,256,256]{2,1,0:T(8,128)} %probe.3) | copy-start | bytes 1572868
  22.8 21.5 %copy-start.3 = (bf16[512,512]{1,0:T(8,128)(2,1)S(1)}, bf16[512,512]{1,0:T(8,128)(2,1)}, u32[]{:S(2)}) copy-start(bf16[512,512]{1,0:T(8,128)(2,1)} %constant.209.clone.bl) | copy-start | bytes 1572868
  22.8 21.5 %copy-start.5 = (bf16[512,512]{1,0:T(8,128)(2,1)S(1)}, bf16[512,512]{1,0:T(8,128)(2,1)}, u32[]{:S(2)}) copy-start(bf16[512,512]{1,0:T(8,128)(2,1)} %constant.208.clone.bh) | copy-start | bytes 1572868
  22.8 21.5 %copy-start.7 = (bf16[512,512]{1,0:T(8,128)(2,1)S(1)}, bf16[512,512]{1,0:T(8,128)(2,1)}, u32[]{:S(2)}) copy-start(bf16[512,512]{1,0:T(8,128)(2,1)} %constant.207.clone.al) | copy-start | bytes 1572868
  64.5 7.7 %copy-start.11 = (f32[6,256,256]{2,1,0:T(8,128)}, f32[6,256,256]{2,1,0:T(8,128)S(1)}, u32[]{:S(2)}) copy-start(f32[6,256,256]{2,1,0:T(8,128)S(1)} %get-tuple-element.103) | copy-start | bytes 4718596
  64.6 7.6 %collective-permute-start.4 = (f32[2,128,512]{2,1,0:T(8,128)S(1)}, f32[2,128,512]{2,1,0:T(8,128)S(1)}, u32[]{:S(2)}, u32[]{:S(2)}) collective-permute-start(f32[2,128,512]{2,1,0:T(8,128)S(1)} %get-tuple-element.109), channel_id=1, source_target_pairs={{4,0},{8,4},{12,8},{16,12},{20,16},{24,20},{28,24},{5,1},{9,5},{13... | collective-permute-start | bytes 1572872 | tf_op jit(solution)/shard_map/ppermute | solution.py:23
  65.9 7.7 %collective-permute-start.5 = (f32[2,128,512]{2,1,0:T(8,128)S(1)}, f32[2,128,512]{2,1,0:T(8,128)S(1)}, u32[]{:S(2)}, u32[]{:S(2)}) collective-permute-start(f32[2,128,512]{2,1,0:T(8,128)S(1)} %get-tuple-element.108), channel_id=1, source_target_pairs={{0,4},{4,8},{8,12},{12,16},{16,20},{20,24},{24,28},{1,5},{5,9},{9,... | collective-permute-start | bytes 1572872 | tf_op jit(solution)/shard_map/ppermute | solution.py:23
  73.9 8.3 %collective-permute-start.6 = (f32[2,256,128]{2,1,0:T(8,128)S(1)}, f32[2,256,128]{2,1,0:T(8,128)S(1)}, u32[]{:S(2)}, u32[]{:S(2)}) collective-permute-start(f32[2,256,128]{2,1,0:T(8,128)S(1)} %get-tuple-element.115), channel_id=1, source_target_pairs={{1,0},{2,1},{3,2},{5,4},{6,5},{7,6},{9,8},{10,9},{11,10},{13,12},{... | collective-permute-start | bytes 786440 | tf_op jit(solution)/shard_map/ppermute | solution.py:23
  75.2 8.4 %collective-permute-start.7 = (f32[2,256,128]{2,1,0:T(8,128)S(1)}, f32[2,256,128]{2,1,0:T(8,128)S(1)}, u32[]{:S(2)}, u32[]{:S(2)}) collective-permute-start(f32[2,256,128]{2,1,0:T(8,128)S(1)} %get-tuple-element.114), channel_id=1, source_target_pairs={{0,1},{1,2},{2,3},{4,5},{5,6},{6,7},{8,9},{9,10},{10,11},{12,13},{... | collective-permute-start | bytes 786440 | tf_op jit(solution)/shard_map/ppermute | solution.py:23
  142.0 6.1 %copy-start.12 = (f32[2,256,256]{2,1,0:T(8,128)}, f32[2,256,256]{2,1,0:T(8,128)S(1)}, u32[]{:S(2)}) copy-start(f32[2,256,256]{2,1,0:T(8,128)S(1)} %divide_subtract_fusion.1) | copy-start | bytes 1572868
  142.9 2.7 collective-permute-start.8
  144.2 3.8 collective-permute-start.9
  145.6 311.3 %all-reduce.5.cloned.1.call-start = ((), (), s32[]{:S(2)}) async-start(), calls=%async_computation.1 | async-start | bytes 3145728 | tf_op jit(solution)/shard_map/psum | solution.py:164
  148.0 1.1 copy-start.16
  149.2 133.2 %collective-permute-start.10 = (f32[2,512,128]{2,1,0:T(8,128)}, f32[2,512,128]{2,1,0:T(8,128)}, u32[]{:S(2)}, u32[]{:S(2)}) collective-permute-start(f32[2,512,128]{2,1,0:T(8,128)} %get-tuple-element.112), channel_id=1, source_target_pairs={{0,1},{1,2},{2,3},{4,5},{5,6},{6,7},{8,9},{9,10},{10,11},{12,13},{... | collective-permute-start | bytes 1572872 | tf_op jit(solution)/shard_map/ppermute | solution.py:31
  154.1 128.3 %collective-permute-start.11 = (f32[2,512,128]{2,1,0:T(8,128)}, f32[2,512,128]{2,1,0:T(8,128)}, u32[]{:S(2)}, u32[]{:S(2)}) collective-permute-start(f32[2,512,128]{2,1,0:T(8,128)} %get-tuple-element.113), channel_id=1, source_target_pairs={{1,0},{2,1},{3,2},{5,4},{6,5},{7,6},{9,8},{10,9},{11,10},{13,12},{... | collective-permute-start | bytes 1572872 | tf_op jit(solution)/shard_map/ppermute | solution.py:34
  280.7 1.7 copy-start.13
  280.7 1.7 copy-start.17
  282.3 1.6 copy-start.4
  282.4 1.6 copy-start.6
  282.4 1.7 copy-start.8
  282.4 1.8 copy-start.10
  305.6 4.5 collective-permute-start.12
  306.9 4.6 collective-permute-start.13
  312.4 8.5 %collective-permute-start.14 = (f32[2,256,128]{2,1,0:T(8,128)}, f32[2,256,128]{2,1,0:T(8,128)S(1)}, u32[]{:S(2)}, u32[]{:S(2)}) collective-permute-start(f32[2,256,128]{2,1,0:T(8,128)} %get-tuple-element.111), channel_id=1, source_target_pairs={{1,0},{2,1},{3,2},{5,4},{6,5},{7,6},{9,8},{10,9},{11,10},{13,12},{... | collective-permute-start | bytes 786440 | tf_op jit(solution)/shard_map/ppermute | solution.py:23
  313.7 8.7 %collective-permute-start.15 = (f32[2,256,128]{2,1,0:T(8,128)}, f32[2,256,128]{2,1,0:T(8,128)S(1)}, u32[]{:S(2)}, u32[]{:S(2)}) collective-permute-start(f32[2,256,128]{2,1,0:T(8,128)} %get-tuple-element.110), channel_id=1, source_target_pairs={{0,1},{1,2},{2,3},{4,5},{5,6},{6,7},{8,9},{9,10},{10,11},{12,13},{... | collective-permute-start | bytes 786440 | tf_op jit(solution)/shard_map/ppermute | solution.py:23
  318.3 57.7 %copy-start.14 = (f32[2,256,256]{2,1,0:T(8,128)S(1)}, f32[2,256,256]{2,1,0:T(8,128)}, u32[]{:S(2)}) copy-start(f32[2,256,256]{2,1,0:T(8,128)} %copy-done.12) | copy-start | bytes 1572868
Sparse Core Ops, SparseCore 0:
  145.7 135.0 all-reduce.2
  318.4 138.3 all-reduce.4
where the time goes:
time: 467 us; the launch traced here: 466 us
  waiting for transfers between devices  241 us (52%)
  blocking collectives  108 us (23%)
  starting transfers between devices  41.6 us (9%)
  Pallas kernels  41.6 us (9%)
  between operations  16 us (3%)
  other arithmetic  11.5 us (2%)
  local copies, waits for them, and re-layouts  6.58 us (1%)
    psum x2, waiting for transfers between devices, local(): stats = lax.psum(stats, ('row', 'col'))  205 us
    psum x2, blocking collectives, local(): sumsq = lax.psum(jnp.sum(grad * grad), ('row', 'col'))  108 us
    pallas_call x2, Pallas kernels, visit_windows(): pl.pallas_call(visit_kernel, out_shape=(jax.ShapeDtypeStruct(ext.shape, j...  41.6 us
    ppermute x8, starting transfers between devices, passed_along(): return lax.ppermute(block, axis, route)  23.6 us
    ppermute x4, waiting for transfers between devices, padded(): lax.ppermute(lax.slice_in_dim(block, 0, width, axis=dim), axis, backward)  18.8 us
    ppermute x4, starting transfers between devices, padded(): lax.ppermute(lax.slice_in_dim(block, block.shape[dim] - width, None, axis...  12.8 us
    ppermute x8, waiting for transfers between devices, passed_along(): return lax.ppermute(block, axis, route)  10.4 us
  transfers between devices with their start and end apart: 18, of which 12 were waited for; matrix products, arithmetic and copies ran while one was open for 1% of the time, Pallas kernels for 0%

commit v1 on v0

--- a/solution.py
+++ b/solution.py
@@ -15,25 +15,6 @@
 STEP_RATE = 0.2
 RIDGE = 1.0
 EPSILON = 1e-06
-
-
-def passed_along(block, axis, distance):
-    devices = range(lax.axis_size(axis))
-    route = [(i - distance, i) for i in devices if i - distance in devices]
-    return lax.ppermute(block, axis, route)
-
-
-def padded(block, sides, width):
-    for axis, dim in sides:
-        count = lax.axis_size(axis)
-        forward = [(i, i + 1) for i in range(count - 1)]
-        backward = [(target, source) for source, target in forward]
-        low = lax.ppermute(
-            lax.slice_in_dim(block, block.shape[dim] - width, None, axis=dim), axis, forward
-        )
-        high = lax.ppermute(lax.slice_in_dim(block, 0, width, axis=dim), axis, backward)
-        block = jnp.concatenate([low, block, high], axis=dim)
-    return block
 
 
 def dft_stacks(order):
@@ -133,41 +114,351 @@
     )(offs, ext, probe, coeffs, pats, *stacks)
 
 
-def fold_rows(grad_ext, half):
-    received = []
-    for toward, border in ((-1, grad_ext[:, :half, :]), (1, grad_ext[:, -half:, :])):
-        received.append(passed_along(border, "row", toward))
-    middle = grad_ext[:, half:-half, :]
-    return middle.at[:, -half:, :].add(received[0]).at[:, :half, :].add(received[1])
-
-
-def fold_cols(grad_mid, half):
-    received = []
-    for toward, border in ((-1, grad_mid[:, :, :half]), (1, grad_mid[:, :, -half:])):
-        received.append(passed_along(border, "col", toward))
-    middle = grad_mid[:, :, half:-half]
-    return middle.at[:, :, -half:].add(received[0]).at[:, :, :half].add(received[1])
+class Link:
+    def __init__(self, axis, step, source, target, sems, slot):
+        self.axis, self.step = axis, step
+        here, count = lax.axis_index(axis), lax.axis_size(axis)
+        self.copy = remote(
+            source, target, sems, slot, {axis: lax.rem(here + step + count, count)}
+        )
+
+    def exists(self, step):
+        here, count = lax.axis_index(self.axis), lax.axis_size(self.axis)
+        return here > 0 if step < 0 else here < count - 1
+
+    def start(self):
+        pl.when(self.exists(self.step))(self.copy.start)
+        return self
+
+    def arrived(self, then=None):
+        @pl.when(self.exists(-self.step))
+        def _():
+            self.copy.wait_recv()
+            if then is not None:
+                then()
+
+    def sent(self):
+        pl.when(self.exists(self.step))(self.copy.wait_send)
+
+
+def remote(source, target, sems, slot, device):
+    send, recv = sems
+    where = tuple(device.get(axis, lax.axis_index(axis)) for axis in ("row", "col"))
+    return pltpu.make_async_remote_copy(
+        src_ref=source,
+        dst_ref=target,
+        send_sem=send.at[slot],
+        recv_sem=recv.at[slot],
+        device_id=where,
+        device_id_type=pl.DeviceIdType.MESH,
+    )
+
+
+def greet():
+    barrier = pltpu.get_barrier_semaphore()
+    count = 0
+    for axis in ("row", "col"):
+        size = lax.axis_size(axis)
+        here = lax.axis_index(axis)
+        for distance in range(1, size):
+            other = {"row": lax.axis_index("row"), "col": lax.axis_index("col")}
+            other[axis] = lax.rem(here + distance, size)
+            pl.semaphore_signal(
+                barrier,
+                inc=1,
+                device_id=(other["row"], other["col"]),
+                device_id_type=pl.DeviceIdType.MESH,
+            )
+            count += 1
+    pl.semaphore_wait(barrier, count)
+
+
+class Slots:
+    def __init__(self, sems):
+        self.sems, self.used = sems, 0
+
+    def next(self):
+        self.used += 1
+        return self.used - 1
+
+
+def copies_needed():
+    rows, cols = lax.axis_size("row"), lax.axis_size("col")
+    return 2 * (1 + cols + rows // 2) + cols + rows + 8
+
+
+def halo_cols(field, half, tile, slots):
+    inner = pl.ds(half, tile)
+    return [
+        Link("col", -1, field.at[:, inner, half : 2 * half],
+             field.at[:, inner, half + tile :], slots.sems, slots.next()).start(),
+        Link("col", 1, field.at[:, inner, tile : half + tile],
+             field.at[:, inner, :half], slots.sems, slots.next()).start(),
+    ]
+
+
+def halo_rows(field, half, tile, slots):
+    return [
+        Link("row", -1, field.at[:, half : 2 * half, :],
+             field.at[:, half + tile :, :], slots.sems, slots.next()).start(),
+        Link("row", 1, field.at[:, tile : half + tile, :],
+             field.at[:, :half, :], slots.sems, slots.next()).start(),
+    ]
+
+
+def update_kernel(last, grad, stats, field, coeffs, field_out, coeffs_out,
+                  gfull, from_rows, mid, from_cols, half_sums, col_sums, shard, z_sums,
+                  new_coeffs, sq_mine, sq_cols, sq_part, sq_rows, send, recv):
+    rows, cols = lax.axis_size("row"), lax.axis_size("col")
+    r, c = lax.axis_index("row"), lax.axis_index("col")
+    depth = rows // 2
+    k, z = lax.rem(r, 2), lax.div(r, 2)
+    width = stats.shape[1]
+    half = width // 2
+    tile = grad.shape[1] - width
+    slots = Slots((send, recv))
+    rows1, rows2, rows3 = half_sums.shape[1], shard.shape[1], z_sums.shape[2]
+    cut = rows3 < rows2
+
+    gfull[...] = jnp.zeros_like(gfull)
+    greet()
+
+    def at(start, size):
+        return pl.ds(pl.multiple_of(start, 8), size)
+
+    def to(source, target, device):
+        copy = remote(source, target, slots.sems, slots.next(), device)
+        copy.start()
+        return copy
+
+    waiting = []
+    low = Link("row", -1, grad.at[:, :half, :], from_rows.at[0], slots.sems, slots.next()).start()
+    high = Link("row", 1, grad.at[:, half + tile :, :], from_rows.at[1], slots.sems, slots.next()).start()
+    waiting += [low.sent, high.sent]
+    partner = {"row": r + 1 - 2 * k}
+    pair = to(stats.at[:, at((1 - k) * rows1, rows1), :], half_sums, partner)
+    waiting.append(pair.wait_send)
+
+    mid[...] = grad[:, half : half + tile, :]
+
+    def add_low():
+        mid[:, tile - half :, :] += from_rows[0]
+
+    def add_high():
+        mid[:, :half, :] += from_rows[1]
+
+    low.arrived(add_low)
+    high.arrived(add_high)
+    low = Link("col", -1, mid.at[:, :, :half], from_cols.at[0], slots.sems, slots.next()).start()
+    high = Link("col", 1, mid.at[:, :, half + tile :], from_cols.at[1], slots.sems, slots.next()).start()
+    waiting += [low.sent, high.sent]
+
+    pair.wait_recv()
+    half_sums[...] += stats[:, at(k * rows1, rows1), :]
+    over_cols = []
+    for d in range(1, cols):
+        other = lax.rem(c + d, cols)
+        over_cols.append(
+            to(half_sums.at[:, at(other * rows2, rows2), :], col_sums.at[d - 1], {"col": other})
+        )
+
+    inner = pl.ds(half, tile)
+    gfull[:, inner, half : half + tile] = mid[:, :, half : half + tile]
+
+    def add_low():
+        gfull[:, inner, tile : half + tile] += from_cols[0]
+
+    def add_high():
+        gfull[:, inner, half : 2 * half] += from_cols[1]
+
+    low.arrived(add_low)
+    high.arrived(add_high)
+    if not last:
+        links = halo_cols(gfull, half, tile, slots)
+    mine = gfull[:, inner, half : half + tile]
+    square = jnp.sum(mine * mine, axis=0)
+    square = jnp.sum(square.reshape(-1, 8, tile), axis=0)
+    sq_mine[...] = sum(square[:, i : i + 128] for i in range(0, tile, 128))
+    sq_over_cols = [
+        to(sq_mine, sq_cols.at[d - 1], {"col": lax.rem(c + d, cols)}) for d in range(1, cols)
+    ]
+    for copy in sq_over_cols:
+        copy.wait_recv()
+    sq_part[...] = sq_mine[...] + sum(sq_cols[d] for d in range(cols - 1))
+    sq_over_rows = [
+        to(sq_part, sq_rows.at[d - 1], {"row": lax.rem(r + d, rows)}) for d in range(1, rows)
+    ]
+    if not last:
+        for link in links:
+            link.arrived()
+        waiting += [link.sent for link in links]
+        links = halo_rows(gfull, half, tile, slots)
+        waiting += [link.sent for link in links]
+
+    for copy in over_cols:
+        copy.wait_recv()
+    shard[...] = half_sums[:, at(c * rows2, rows2), :] + sum(col_sums[d] for d in range(cols - 1))
+    over_z = []
+    for d in range(1, depth):
+        other = lax.rem(z + d, depth)
+        source = shard.at[:, at(other * rows3, rows3), :] if cut else shard
+        over_z.append(to(source, z_sums.at[z], {"row": 2 * other + k}))
+    z_sums[z] = shard[:, at(z * rows3, rows3), :] if cut else shard[...]
+    for copy in over_z:
+        copy.wait_recv()
+    sums = sum(z_sums[i] for i in range(depth))
+    base2 = k * rows1 + c * rows2
+    base3 = base2 + z * rows3 if cut else base2
+    new_coeffs[:, at(base3, rows3), :] = coeffs[:, at(base3, rows3), :] - sums[:3] / (sums[3:] + RIDGE)
+    back = []
+    if cut:
+        ready = new_coeffs.at[:, at(base3, rows3), :]
+        for d in range(1, depth):
+            back.append(to(ready, ready, {"row": 2 * lax.rem(z + d, depth) + k}))
+        for copy in back:
+            copy.wait_recv()
+    ready = new_coeffs.at[:, at(base2, rows2), :]
+    wide = [to(ready, ready, {"col": lax.rem(c + d, cols)}) for d in range(1, cols)]
+    for copy in wide:
+        copy.wait_recv()
+    ready = new_coeffs.at[:, at(k * rows1, rows1), :]
+    pair = to(ready, ready, partner)
+
+    for copy in sq_over_rows:
+        copy.wait_recv()
+    square = sq_part[...] + sum(sq_rows[d] for d in range(rows - 1))
+    total = 2.0 * tile * tile * rows * cols
+    rate = STEP_RATE / jnp.sqrt(jnp.sum(square, keepdims=True) / total + EPSILON)
+    if last:
+        for part in (0, 1):
+            field_out[part] = field[part, inner, half : half + tile] - rate * gfull[part, inner, half : half + tile]
+    else:
+        for link in links:
+            link.arrived()
+        for part in (0, 1):
+            field_out[part] = field[part] - rate * gfull[part]
+    pair.wait()
+    coeffs_out[...] = new_coeffs[...]
+    for done in waiting:
+        done()
+    for copy in over_cols + sq_over_cols + sq_over_rows + over_z + back + wide:
+        copy.wait_send()
+
+
+def update(last, grad, stats, field, coeffs):
+    rows, cols = lax.axis_size("row"), lax.axis_size("col")
+    depth = rows // 2
+    size, width = grad.shape[1], stats.shape[1]
+    half, tile = width // 2, size - width
+    rows1 = width // 2
+    rows2 = rows1 // cols
+    rows3 = rows2 // depth if rows2 % (8 * depth) == 0 else rows2
+    vmem = pl.BlockSpec(memory_space=pltpu.VMEM)
+    f32 = jnp.float32
+    count = copies_needed()
+    side = tile if last else size
+    return pl.pallas_call(
+        functools.partial(update_kernel, last),
+        out_shape=(
+            jax.ShapeDtypeStruct((2, side, side), f32),
+            jax.ShapeDtypeStruct(coeffs.shape, f32),
+        ),
+        in_specs=[vmem] * 4,
+        out_specs=(vmem, vmem),
+        scratch_shapes=[
+            pltpu.VMEM((2, size, size), f32),
+            pltpu.VMEM((2, 2, half, size), f32),
+            pltpu.VMEM((2, tile, size), f32),
+            pltpu.VMEM((2, 2, tile, half), f32),
+            pltpu.VMEM((6, rows1, width), f32),
+            pltpu.VMEM((cols - 1, 6, rows2, width), f32),
+            pltpu.VMEM((6, rows2, width), f32),
+            pltpu.VMEM((depth, 6, rows3, width), f32),
+            pltpu.VMEM(coeffs.shape, f32),
+            pltpu.VMEM((8, 128), f32),
+            pltpu.VMEM((cols - 1, 8, 128), f32),
+            pltpu.VMEM((8, 128), f32),
+            pltpu.VMEM((rows - 1, 8, 128), f32),
+            pltpu.SemaphoreType.DMA((count,)),
+            pltpu.SemaphoreType.DMA((count,)),
+        ],
+        compiler_params=pltpu.CompilerParams(
+            collective_id=2 if last else 1,
+            has_side_effects=True,
+            vmem_limit_bytes=48 * 1024 * 1024,
+        ),
+        name="update_last" if last else "update",
+    )(grad, stats, field, coeffs)
+
+
+def extend_kernel(half, tile, field, out, full, send, recv):
+    full[...] = jnp.zeros_like(full)
+    inner = pl.ds(half, tile)
+    full[:, inner, half : half + tile] = field[...]
+    barrier = pltpu.get_barrier_semaphore()
+    count = jnp.int32(0)
+    for axis in ("row", "col"):
+        size = lax.axis_size(axis)
+        here = lax.axis_index(axis)
+        for step in (-1, 1):
+            other = {"row": lax.axis_index("row"), "col": lax.axis_index("col")}
+            other[axis] = lax.rem(here + step + size, size)
+            exists = here > 0 if step < 0 else here < size - 1
+            count += exists.astype(jnp.int32)
+
+            @pl.when(exists)
+            def _():
+                pl.semaphore_signal(
+                    barrier,
+                    inc=1,
+                    device_id=(other["row"], other["col"]),
+                    device_id_type=pl.DeviceIdType.MESH,
+                )
+
+    pl.semaphore_wait(barrier, count)
+    slots = Slots((send, recv))
+    side = halo_cols(full, half, tile, slots)
+    for link in side:
+        link.arrived()
+    ends = halo_rows(full, half, tile, slots)
+    for link in ends:
+        link.arrived()
+    out[...] = full[...]
+    for link in side + ends:
+        link.sent()
+
+
+def extend(field, half):
+    tile = field.shape[1]
+    size = tile + 2 * half
+    vmem = pl.BlockSpec(memory_space=pltpu.VMEM)
+    return pl.pallas_call(
+        functools.partial(extend_kernel, half, tile),
+        out_shape=jax.ShapeDtypeStruct((2, size, size), jnp.float32),
+        in_specs=[vmem],
+        out_specs=vmem,
+        scratch_shapes=[
+            pltpu.VMEM((2, size, size), jnp.float32),
+            pltpu.SemaphoreType.DMA((4,)),
+            pltpu.SemaphoreType.DMA((4,)),
+        ],
+        compiler_params=pltpu.CompilerParams(
+            collective_id=0, has_side_effects=True, vmem_limit_bytes=32 * 1024 * 1024
+        ),
+        name="extend",
+    )(field)
 
 
 def local(object_field, probe, coeffs, patterns, offsets):
     width = probe.shape[1]
-    half = width // 2
-    tile = object_field.shape[1]
     stacks = dft_stacks(width)
     flat_pats = patterns.reshape(-1, width, width)
     flat_offs = offsets.reshape(-1, 2)
-    devices = lax.axis_size("row") * lax.axis_size("col")
-    total = 2.0 * tile * tile * devices
+    field = extend(object_field, width // 2)
     for turn in range(ITERS):
-        extended = padded(object_field, (("row", 1), ("col", 2)), half)
-        grad_ext, stats = visit_windows(flat_offs, extended, probe, coeffs, flat_pats, stacks)
-        stats = lax.psum(stats, ("row", "col"))
-        new_coeffs = coeffs - stats[:3] / (stats[3:] + RIDGE)
-        grad = fold_cols(fold_rows(grad_ext, half), half)
-        sumsq = lax.psum(jnp.sum(grad * grad), ("row", "col"))
-        object_field = object_field - STEP_RATE * grad / jnp.sqrt(sumsq / total + EPSILON)
-        coeffs = new_coeffs
-    return (object_field, coeffs)
+        grad, stats = visit_windows(flat_offs, field, probe, coeffs, flat_pats, stacks)
+        field, coeffs = update(turn == ITERS - 1, grad, stats, field, coeffs)
+    return (field, coeffs)
 
 
 def solution(mesh):

time: 467 us -> 193 us (0.41)
  waiting for transfers between devices: 241 us -> 0 us
  Pallas kernels: 41.6 us -> 182 us
  blocking collectives: 108 us -> 0 us
  starting transfers between devices: 41.6 us -> 0 us
  between operations: 16 us -> 0.8 us
  other arithmetic: 11.5 us -> 0 us
    psum x2 -> x0, waiting for transfers between devices: 205 us -> none  [local(): stats = lax.psum(stats, ('row', 'col'))]
    pallas_call x0 -> x3, Pallas kernels: none -> 142 us  [the longest x2 129 us: update(): pl.pallas_call(functools.partial(update_kernel, last), out_shape=(jax.Sha...]
    psum x2 -> x0, blocking collectives: 108 us -> none  [local(): sumsq = lax.psum(jnp.sum(grad * grad), ('row', 'col'))]
    ppermute x16 -> x0, starting transfers between devices: 41.6 us -> none  [the longest x8 23.6 us: passed_along(): return lax.ppermute(block, axis, route)]
    ppermute x16 -> x0, waiting for transfers between devices: 35.7 us -> none  [the longest x4 18.8 us: padded(): lax.ppermute(lax.slice_in_dim(block, 0, width, axis=dim), axis, backward)]
    unnamed x40 -> x32, local copies, waits for them, and re-layouts: 1.37 us -> 8.24 us
    sub x4 -> x0, other arithmetic: 5.98 us -> none  [the longest x2 4 us: local(): new_coeffs = coeffs - stats[:3] / (stats[3:] + RIDGE)]
    slice x12 -> x0, local copies, waits for them, and re-layouts: 5.1 us -> none  [the longest x3 2.83 us: padded(): lax.slice_in_dim(block, block.shape[dim] - width, None, axis=dim)]
  transfers between devices with their start and end apart: 18 -> 0, of which waited for: 12 -> 0; matrix products, arithmetic and copies ran while one was open for 1% -> 0% of each run, Pallas kernels for 0% -> 0%
where the time goes in v1:
time: 193 us; the launch traced here: 192 us
  Pallas kernels  182 us (94%)
  local copies, waits for them, and re-layouts  9.16 us (5%)
    pallas_call x2, Pallas kernels, update(): pl.pallas_call(functools.partial(update_kernel, last), out_shape=(jax.Sha...  129 us
    pallas_call x2, Pallas kernels, visit_windows(): pl.pallas_call(visit_kernel, out_shape=(jax.ShapeDtypeStruct(ext.shape, j...  40 us
    pallas_call x1, Pallas kernels, extend(): pl.pallas_call(functools.partial(extend_kernel, half, tile), out_shape=ja...  13.3 us
    unnamed x32, local copies, waits for them, and re-layouts  8.24 us

profile of v1, /device:TPU:0, one launch (start us, length us, event | category | flops | bytes accessed | tf_op | source)
XLA Modules:
  0.0 192.1 jit_solution(15776750718407972123)
XLA Ops:
  0.6 0.0 copy-start.3
  0.6 0.0 copy-start.5
  0.7 0.0 copy-start.2
  0.7 0.9 copy.12.offs
  1.6 0.0 copy-start.14
  1.6 1.0 copy-done.14
  2.6 13.3 %extend.1.ext.field = f32[2,512,512]{2,1,0:T(8,128)S(1)} custom-call(f32[2,256,256]{2,1,0:T(8,128)S(1)} %copy-done.14), custom_call_target="tpu_custom_call" | custom-call | tf_op jit(solution)/shard_map/extend/pallas_call | solution.py:435
  15.9 0.0 copy-done.3
  15.9 0.0 copy-done.5
  15.9 0.0 copy-done.2
  15.9 0.0 copy-start.6
  15.9 1.0 copy-done.6
  17.0 0.0 copy-start.8
  17.0 1.0 copy-done.8
  18.0 0.0 copy-start.10
  18.0 1.0 copy-done.10
  19.1 0.0 copy-start.12
  19.1 1.0 copy-done.12
  20.1 0.0 copy-start
  20.1 20.0 %visit_windows.2 = (f32[2,512,512]{2,1,0:T(8,128)S(1)}, f32[6,256,256]{2,1,0:T(8,128)S(1)}) custom-call(s32[4,2]{1,0:T(4,128)S(1)} %copy.12.offs, f32[2,512,512]{2,1,0:T(8,128)S(1)} %extend.1.ext.field, f32[2,256,256]{2,1,0:T(8,128)S(1)} %copy-done.5, f32[3,256,256]{2,1,0:T(8,128)S(1)} %copy-done.3, f32[4,256,256]{2,1,0:T(8,128)S(1)} %bitcast.2, ...), custom_call_target="tpu_custom_call" | custom-call | tf_op jit(solution)/shard_map/visit_windows/pallas_call | solution.py:103
  40.1 0.0 copy-done
  40.1 0.0 copy-start.4
  40.1 1.3 copy-done.4
  41.5 0.0 copy-start.7
  41.5 0.0 copy-start.9
  41.5 0.0 copy-start.11
  41.5 0.0 copy-start.13
  41.5 80.5 %update.1 = (f32[2,512,512]{2,1,0:T(8,128)S(1)}, f32[3,256,256]{2,1,0:T(8,128)S(1)}) custom-call(f32[2,512,512]{2,1,0:T(8,128)} %copy-done.4, f32[6,256,256]{2,1,0:T(8,128)S(1)} %get-tuple-element.9.stats, f32[2,512,512]{2,1,0:T(8,128)} %copy-done, f32[3,256,256]{2,1,0:T(8,128)S(1)} %copy-done.3), custom_call_target="tpu_custom_call" | custom-call | tf_op jit(solution)/shard_map/update/pallas_call | solution.py:360
  122.0 0.0 copy-start.1
  122.0 0.0 copy-done.7
  122.0 0.0 copy-done.9
  122.0 0.0 copy-done.11
  122.0 0.0 copy-done.13
  122.0 20.0 %visit_windows.3 = (f32[2,512,512]{2,1,0:T(8,128)S(1)}, f32[6,256,256]{2,1,0:T(8,128)S(1)}) custom-call(s32[4,2]{1,0:T(4,128)S(1)} %copy.12.offs, f32[2,512,512]{2,1,0:T(8,128)S(1)} %get-tuple-element.10.ext.field, f32[2,256,256]{2,1,0:T(8,128)S(1)} %copy-done.5, f32[3,256,256]{2,1,0:T(8,128)S(1)} %get-tuple-element.11.coeffs, f32[4,256,256]{2,1,0:T(8,128)S(1)} %bitcast.3, ...), custom_call_target="tpu_custom_call" | custom-call | tf_op jit(solution)/shard_map/visit_windows/pallas_call | solution.py:103
  142.0 0.0 copy-done.1
  142.0 48.4 %update_last.1 = (f32[2,256,256]{2,1,0:T(8,128)S(1)}, f32[3,256,256]{2,1,0:T(8,128)S(1)}) custom-call(f32[2,512,512]{2,1,0:T(8,128)S(1)} %get-tuple-element.12.grad, f32[6,256,256]{2,1,0:T(8,128)S(1)} %get-tuple-element.13.stats, f32[2,512,512]{2,1,0:T(8,128)} %copy-done.1, f32[3,256,256]{2,1,0:T(8,128)S(1)} %get-tuple-element.11.coeffs), custom_call_target="tpu_custom_call" | custom-call | tf_op jit(solution)/shard_map/update_last/pallas_call | solution.py:360
  190.5 0.8 copy.15
  191.3 0.9 copy.16
Async XLA Ops:
  0.6 15.3 %copy-start.3 = (f32[3,256,256]{2,1,0:T(8,128)S(1)}, f32[3,256,256]{2,1,0:T(8,128)}, u32[]{:S(2)}) copy-start(f32[3,256,256]{2,1,0:T(8,128)} %coeffs.3) | copy-start | bytes 2359300
  0.6 15.3 %copy-start.5 = (f32[2,256,256]{2,1,0:T(8,128)S(1)}, f32[2,256,256]{2,1,0:T(8,128)}, u32[]{:S(2)}) copy-start(f32[2,256,256]{2,1,0:T(8,128)} %probe.3) | copy-start | bytes 1572868
  0.7 15.3 %copy-start.2 = (f32[1,1,4,256,256]{4,3,2,1,0:T(8,128)S(1)}, f32[1,1,4,256,256]{4,3,2,1,0:T(8,128)}, u32[]{:S(2)}) copy-start(f32[1,1,4,256,256]{4,3,2,1,0:T(8,128)} %param.12) | copy-start | bytes 3145732
  1.6 1.0 copy-start.14
  15.9 1.0 copy-start.6
  17.0 1.0 copy-start.8
  18.0 1.0 copy-start.10
  19.1 1.0 copy-start.12
  20.1 20.0 %copy-start = (f32[2,512,512]{2,1,0:T(8,128)}, f32[2,512,512]{2,1,0:T(8,128)S(1)}, u32[]{:S(2)}) copy-start(f32[2,512,512]{2,1,0:T(8,128)S(1)} %extend.1.ext.field) | copy-start | bytes 6291460
  40.1 1.3 copy-start.4
  41.5 80.5 %copy-start.7 = (bf16[512,512]{1,0:T(8,128)(2,1)S(1)}, bf16[512,512]{1,0:T(8,128)(2,1)}, u32[]{:S(2)}) copy-start(bf16[512,512]{1,0:T(8,128)(2,1)} %constant.11.clone.bl) | copy-start | bytes 1572868
  41.5 80.6 %copy-start.9 = (bf16[512,512]{1,0:T(8,128)(2,1)S(1)}, bf16[512,512]{1,0:T(8,128)(2,1)}, u32[]{:S(2)}) copy-start(bf16[512,512]{1,0:T(8,128)(2,1)} %constant.10.clone.bh) | copy-start | bytes 1572868
  41.5 80.6 %copy-start.11 = (bf16[512,512]{1,0:T(8,128)(2,1)S(1)}, bf16[512,512]{1,0:T(8,128)(2,1)}, u32[]{:S(2)}) copy-start(bf16[512,512]{1,0:T(8,128)(2,1)} %constant.9.clone.al) | copy-start | bytes 1572868
  41.5 80.6 %copy-start.13 = (bf16[512,512]{1,0:T(8,128)(2,1)S(1)}, bf16[512,512]{1,0:T(8,128)(2,1)}, u32[]{:S(2)}) copy-start(bf16[512,512]{1,0:T(8,128)(2,1)} %constant.8.clone.ah) | copy-start | bytes 1572868
  122.0 20.0 %copy-start.1 = (f32[2,512,512]{2,1,0:T(8,128)}, f32[2,512,512]{2,1,0:T(8,128)S(1)}, u32[]{:S(2)}) copy-start(f32[2,512,512]{2,1,0:T(8,128)S(1)} %get-tuple-element.10.ext.field) | copy-start | bytes 6291460

commit v2 on v1

--- a/solution.py
+++ b/solution.py
@@ -184,31 +184,45 @@
 
 def copies_needed():
     rows, cols = lax.axis_size("row"), lax.axis_size("col")
-    return 2 * (1 + cols + rows // 2) + cols + rows + 8
-
-
-def halo_cols(field, half, tile, slots):
+    return 2 * (1 + cols + rows // 2) + cols + rows + 16
+
+
+def halo_cols(field, part, half, tile, slots):
     inner = pl.ds(half, tile)
     return [
-        Link("col", -1, field.at[:, inner, half : 2 * half],
-             field.at[:, inner, half + tile :], slots.sems, slots.next()).start(),
-        Link("col", 1, field.at[:, inner, tile : half + tile],
-             field.at[:, inner, :half], slots.sems, slots.next()).start(),
+        Link("col", -1, field.at[part, inner, half : 2 * half],
+             field.at[part, inner, half + tile :], slots.sems, slots.next()).start(),
+        Link("col", 1, field.at[part, inner, tile : half + tile],
+             field.at[part, inner, :half], slots.sems, slots.next()).start(),
     ]
 
 
-def halo_rows(field, half, tile, slots):
+def halo_rows(field, part, half, tile, slots):
     return [
-        Link("row", -1, field.at[:, half : 2 * half, :],
-             field.at[:, half + tile :, :], slots.sems, slots.next()).start(),
-        Link("row", 1, field.at[:, tile : half + tile, :],
-             field.at[:, :half, :], slots.sems, slots.next()).start(),
+        Link("row", -1, field.at[part, half : 2 * half, :],
+             field.at[part, half + tile :, :], slots.sems, slots.next()).start(),
+        Link("row", 1, field.at[part, tile : half + tile, :],
+             field.at[part, :half, :], slots.sems, slots.next()).start(),
+    ]
+
+
+def fold_rows(grad, into, part, half, tile, slots):
+    return [
+        Link("row", -1, grad.at[part, :half, :], into.at[0, part], slots.sems, slots.next()).start(),
+        Link("row", 1, grad.at[part, half + tile :, :], into.at[1, part], slots.sems, slots.next()).start(),
+    ]
+
+
+def fold_cols(mid, into, part, half, tile, slots):
+    return [
+        Link("col", -1, mid.at[part, :, :half], into.at[0, part], slots.sems, slots.next()).start(),
+        Link("col", 1, mid.at[part, :, half + tile :], into.at[1, part], slots.sems, slots.next()).start(),
     ]
 
 
 def update_kernel(last, grad, stats, field, coeffs, field_out, coeffs_out,
                   gfull, from_rows, mid, from_cols, half_sums, col_sums, shard, z_sums,
-                  new_coeffs, sq_mine, sq_cols, sq_part, sq_rows, send, recv):
+                  new_coeffs, sq_mine, sq_cols, sq_part, sq_rows, send_sem, recv_sem):
     rows, cols = lax.axis_size("row"), lax.axis_size("col")
     r, c = lax.axis_index("row"), lax.axis_index("col")
     depth = rows // 2
@@ -216,7 +230,7 @@
     width = stats.shape[1]
     half = width // 2
     tile = grad.shape[1] - width
-    slots = Slots((send, recv))
+    slots = Slots((send_sem, recv_sem))
     rows1, rows2, rows3 = half_sums.shape[1], shard.shape[1], z_sums.shape[2]
     cut = rows3 < rows2
 
@@ -231,27 +245,17 @@
         copy.start()
         return copy
 
-    waiting = []
-    low = Link("row", -1, grad.at[:, :half, :], from_rows.at[0], slots.sems, slots.next()).start()
-    high = Link("row", 1, grad.at[:, half + tile :, :], from_rows.at[1], slots.sems, slots.next()).start()
-    waiting += [low.sent, high.sent]
+    links = []
+
+    def send(start, *refs):
+        pair = start(*refs, half, tile, slots)
+        links.extend(pair)
+        return pair
+
+    row_links = [send(fold_rows, grad, from_rows, part) for part in (0, 1)]
     partner = {"row": r + 1 - 2 * k}
     pair = to(stats.at[:, at((1 - k) * rows1, rows1), :], half_sums, partner)
-    waiting.append(pair.wait_send)
-
     mid[...] = grad[:, half : half + tile, :]
-
-    def add_low():
-        mid[:, tile - half :, :] += from_rows[0]
-
-    def add_high():
-        mid[:, :half, :] += from_rows[1]
-
-    low.arrived(add_low)
-    high.arrived(add_high)
-    low = Link("col", -1, mid.at[:, :, :half], from_cols.at[0], slots.sems, slots.next()).start()
-    high = Link("col", 1, mid.at[:, :, half + tile :], from_cols.at[1], slots.sems, slots.next()).start()
-    waiting += [low.sent, high.sent]
 
     pair.wait_recv()
     half_sums[...] += stats[:, at(k * rows1, rows1), :]
@@ -262,38 +266,17 @@
             to(half_sums.at[:, at(other * rows2, rows2), :], col_sums.at[d - 1], {"col": other})
         )
 
-    inner = pl.ds(half, tile)
-    gfull[:, inner, half : half + tile] = mid[:, :, half : half + tile]
-
-    def add_low():
-        gfull[:, inner, tile : half + tile] += from_cols[0]
-
-    def add_high():
-        gfull[:, inner, half : 2 * half] += from_cols[1]
-
-    low.arrived(add_low)
-    high.arrived(add_high)
-    if not last:
-        links = halo_cols(gfull, half, tile, slots)
-    mine = gfull[:, inner, half : half + tile]
-    square = jnp.sum(mine * mine, axis=0)
-    square = jnp.sum(square.reshape(-1, 8, tile), axis=0)
-    sq_mine[...] = sum(square[:, i : i + 128] for i in range(0, tile, 128))
-    sq_over_cols = [
-        to(sq_mine, sq_cols.at[d - 1], {"col": lax.rem(c + d, cols)}) for d in range(1, cols)
-    ]
-    for copy in sq_over_cols:
-        copy.wait_recv()
-    sq_part[...] = sq_mine[...] + sum(sq_cols[d] for d in range(cols - 1))
-    sq_over_rows = [
-        to(sq_part, sq_rows.at[d - 1], {"row": lax.rem(r + d, rows)}) for d in range(1, rows)
-    ]
-    if not last:
-        for link in links:
-            link.arrived()
-        waiting += [link.sent for link in links]
-        links = halo_rows(gfull, half, tile, slots)
-        waiting += [link.sent for link in links]
+    col_links = []
+    for part in (0, 1):
+        def add_low():
+            mid[part, tile - half :, :] += from_rows[0, part]
+
+        def add_high():
+            mid[part, :half, :] += from_rows[1, part]
+
+        row_links[part][0].arrived(add_low)
+        row_links[part][1].arrived(add_high)
+        col_links.append(send(fold_cols, mid, from_cols, part))
 
     for copy in over_cols:
         copy.wait_recv()
@@ -304,6 +287,30 @@
         source = shard.at[:, at(other * rows3, rows3), :] if cut else shard
         over_z.append(to(source, z_sums.at[z], {"row": 2 * other + k}))
     z_sums[z] = shard[:, at(z * rows3, rows3), :] if cut else shard[...]
+
+    inner = pl.ds(half, tile)
+    side_links = []
+    square = 0.0
+    for part in (0, 1):
+        gfull[part, inner, half : half + tile] = mid[part, :, half : half + tile]
+
+        def add_low():
+            gfull[part, inner, tile : half + tile] += from_cols[0, part]
+
+        def add_high():
+            gfull[part, inner, half : 2 * half] += from_cols[1, part]
+
+        col_links[part][0].arrived(add_low)
+        col_links[part][1].arrived(add_high)
+        if not last:
+            side_links.append(send(halo_cols, gfull, part))
+        mine = gfull[part, inner, half : half + tile]
+        square += jnp.sum((mine * mine).reshape(-1, 8, tile), axis=0)
+    sq_mine[...] = sum(square[:, i : i + 128] for i in range(0, tile, 128))
+    sq_over_cols = [
+        to(sq_mine, sq_cols.at[d - 1], {"col": lax.rem(c + d, cols)}) for d in range(1, cols)
+    ]
+
     for copy in over_z:
         copy.wait_recv()
     sums = sum(z_sums[i] for i in range(depth))
@@ -315,14 +322,24 @@
         ready = new_coeffs.at[:, at(base3, rows3), :]
         for d in range(1, depth):
             back.append(to(ready, ready, {"row": 2 * lax.rem(z + d, depth) + k}))
-        for copy in back:
-            copy.wait_recv()
+
+    for copy in sq_over_cols:
+        copy.wait_recv()
+    sq_part[...] = sq_mine[...] + sum(sq_cols[d] for d in range(cols - 1))
+    sq_over_rows = [
+        to(sq_part, sq_rows.at[d - 1], {"row": lax.rem(r + d, rows)}) for d in range(1, rows)
+    ]
+
+    end_links = []
+    if not last:
+        for part in (0, 1):
+            for link in side_links[part]:
+                link.arrived()
+            end_links.append(send(halo_rows, gfull, part))
+    for copy in back:
+        copy.wait_recv()
     ready = new_coeffs.at[:, at(base2, rows2), :]
     wide = [to(ready, ready, {"col": lax.rem(c + d, cols)}) for d in range(1, cols)]
-    for copy in wide:
-        copy.wait_recv()
-    ready = new_coeffs.at[:, at(k * rows1, rows1), :]
-    pair = to(ready, ready, partner)
 
     for copy in sq_over_rows:
         copy.wait_recv()
@@ -332,16 +349,21 @@
     if last:
         for part in (0, 1):
             field_out[part] = field[part, inner, half : half + tile] - rate * gfull[part, inner, half : half + tile]
-    else:
-        for link in links:
-            link.arrived()
+
+    for copy in wide:
+        copy.wait_recv()
+    ready = new_coeffs.at[:, at(k * rows1, rows1), :]
+    final = to(ready, ready, partner)
+    if not last:
         for part in (0, 1):
+            for link in end_links[part]:
+                link.arrived()
             field_out[part] = field[part] - rate * gfull[part]
-    pair.wait()
+    final.wait_recv()
     coeffs_out[...] = new_coeffs[...]
-    for done in waiting:
-        done()
-    for copy in over_cols + sq_over_cols + sq_over_rows + over_z + back + wide:
+    for link in links:
+        link.sent()
+    for copy in [pair, final] + over_cols + sq_over_cols + sq_over_rows + over_z + back + wide:
         copy.wait_send()
 
 
@@ -417,15 +439,19 @@
 
     pl.semaphore_wait(barrier, count)
     slots = Slots((send, recv))
-    side = halo_cols(full, half, tile, slots)
-    for link in side:
-        link.arrived()
-    ends = halo_rows(full, half, tile, slots)
-    for link in ends:
-        link.arrived()
+    side = [halo_cols(full, part, half, tile, slots) for part in (0, 1)]
+    ends = []
+    for part in (0, 1):
+        for link in side[part]:
+            link.arrived()
+        ends.append(halo_rows(full, part, half, tile, slots))
+    for part in (0, 1):
+        for link in ends[part]:
+            link.arrived()
     out[...] = full[...]
-    for link in side + ends:
-        link.sent()
+    for links in side + ends:
+        for link in links:
+            link.sent()
 
 
 def extend(field, half):
@@ -439,8 +465,8 @@
         out_specs=vmem,
         scratch_shapes=[
             pltpu.VMEM((2, size, size), jnp.float32),
-            pltpu.SemaphoreType.DMA((4,)),
-            pltpu.SemaphoreType.DMA((4,)),
+            pltpu.SemaphoreType.DMA((8,)),
+            pltpu.SemaphoreType.DMA((8,)),
         ],
         compiler_params=pltpu.CompilerParams(
             collective_id=0, has_side_effects=True, vmem_limit_bytes=32 * 1024 * 1024

time: 193 us -> 162 us (0.84)
  Pallas kernels: 182 us -> 152 us
    pallas_call x2, Pallas kernels: 129 us -> 96 us  [update(): pl.pallas_call(functools.partial(update_kernel, last), out_shape=(jax.Sha...]
    pallas_call x1, Pallas kernels: 13.3 us -> 15.8 us  [extend(): pl.pallas_call(functools.partial(extend_kernel, half, tile), out_shape=ja...]
where the time goes in v2:
time: 162 us
  Pallas kernels  152 us (94%)
  local copies, waits for them, and re-layouts  9.16 us (6%)
    pallas_call x2, Pallas kernels, update(): pl.pallas_call(functools.partial(update_kernel, last), out_shape=(jax.Sha...  96 us
    pallas_call x2, Pallas kernels, visit_windows(): pl.pallas_call(visit_kernel, out_shape=(jax.ShapeDtypeStruct(ext.shape, j...  40 us
    pallas_call x1, Pallas kernels, extend(): pl.pallas_call(functools.partial(extend_kernel, half, tile), out_shape=ja...  15.8 us
    unnamed x32, local copies, waits for them, and re-layouts  8.24 us

profile of v2, /device:TPU:0, one launch (start us, length us, event | category | flops | bytes accessed | tf_op | source)
XLA Modules:
  0.0 161.7 jit_solution(11448727819999859749)
XLA Ops:
  0.6 0.0 copy-start.3
  0.6 0.0 copy-start.5
  0.7 0.0 copy-start.2
  0.7 0.9 copy.12.offs
  1.6 0.0 copy-start.14
  1.6 1.0 copy-done.14
  2.6 15.8 %extend.1.ext.field = f32[2,512,512]{2,1,0:T(8,128)S(1)} custom-call(f32[2,256,256]{2,1,0:T(8,128)S(1)} %copy-done.14), custom_call_target="tpu_custom_call" | custom-call | tf_op jit(solution)/shard_map/extend/pallas_call | solution.py:461
  18.4 0.0 copy-done.3
  18.4 0.0 copy-done.5
  18.4 0.0 copy-done.2
  18.4 0.0 copy-start.6
  18.4 1.0 copy-done.6
  19.5 0.0 copy-start.8
  19.5 1.0 copy-done.8
  20.5 0.0 copy-start.10
  20.5 1.0 copy-done.10
  21.6 0.0 copy-start.12
  21.6 1.0 copy-done.12
  22.6 0.0 copy-start
  22.6 20.0 %visit_windows.2 = (f32[2,512,512]{2,1,0:T(8,128)S(1)}, f32[6,256,256]{2,1,0:T(8,128)S(1)}) custom-call(s32[4,2]{1,0:T(4,128)S(1)} %copy.12.offs, f32[2,512,512]{2,1,0:T(8,128)S(1)} %extend.1.ext.field, f32[2,256,256]{2,1,0:T(8,128)S(1)} %copy-done.5, f32[3,256,256]{2,1,0:T(8,128)S(1)} %copy-done.3, f32[4,256,256]{2,1,0:T(8,128)S(1)} %bitcast.2, ...), custom_call_target="tpu_custom_call" | custom-call | tf_op jit(solution)/shard_map/visit_windows/pallas_call | solution.py:103
  42.6 0.0 copy-done
  42.6 0.0 copy-start.4
  42.6 1.3 copy-done.4
  44.0 0.0 copy-start.7
  44.0 0.0 copy-start.9
  44.0 0.0 copy-start.11
  44.0 0.0 copy-start.13
  44.0 56.0 %update.1 = (f32[2,512,512]{2,1,0:T(8,128)S(1)}, f32[3,256,256]{2,1,0:T(8,128)S(1)}) custom-call(f32[2,512,512]{2,1,0:T(8,128)} %copy-done.4, f32[6,256,256]{2,1,0:T(8,128)S(1)} %get-tuple-element.9.stats, f32[2,512,512]{2,1,0:T(8,128)} %copy-done, f32[3,256,256]{2,1,0:T(8,128)S(1)} %copy-done.3), custom_call_target="tpu_custom_call" | custom-call | tf_op jit(solution)/shard_map/update/pallas_call | solution.py:382
  100.0 0.0 copy-start.1
  100.0 0.0 copy-done.7
  100.0 0.0 copy-done.9
  100.0 0.0 copy-done.11
  100.0 0.0 copy-done.13
  100.0 20.0 %visit_windows.3 = (f32[2,512,512]{2,1,0:T(8,128)S(1)}, f32[6,256,256]{2,1,0:T(8,128)S(1)}) custom-call(s32[4,2]{1,0:T(4,128)S(1)} %copy.12.offs, f32[2,512,512]{2,1,0:T(8,128)S(1)} %get-tuple-element.10.ext.field, f32[2,256,256]{2,1,0:T(8,128)S(1)} %copy-done.5, f32[3,256,256]{2,1,0:T(8,128)S(1)} %get-tuple-element.11.coeffs, f32[4,256,256]{2,1,0:T(8,128)S(1)} %bitcast.3, ...), custom_call_target="tpu_custom_call" | custom-call | tf_op jit(solution)/shard_map/visit_windows/pallas_call | solution.py:103
  120.0 0.0 copy-done.1
  120.0 40.0 %update_last.1 = (f32[2,256,256]{2,1,0:T(8,128)S(1)}, f32[3,256,256]{2,1,0:T(8,128)S(1)}) custom-call(f32[2,512,512]{2,1,0:T(8,128)S(1)} %get-tuple-element.12.grad, f32[6,256,256]{2,1,0:T(8,128)S(1)} %get-tuple-element.13.stats, f32[2,512,512]{2,1,0:T(8,128)} %copy-done.1, f32[3,256,256]{2,1,0:T(8,128)S(1)} %get-tuple-element.11.coeffs), custom_call_target="tpu_custom_call" | custom-call | tf_op jit(solution)/shard_map/update_last/pallas_call | solution.py:382
  160.0 0.8 copy.15
  160.8 0.9 copy.16
Async XLA Ops:
  0.6 17.8 %copy-start.3 = (f32[3,256,256]{2,1,0:T(8,128)S(1)}, f32[3,256,256]{2,1,0:T(8,128)}, u32[]{:S(2)}) copy-start(f32[3,256,256]{2,1,0:T(8,128)} %coeffs.3) | copy-start | bytes 2359300
  0.6 17.8 %copy-start.5 = (f32[2,256,256]{2,1,0:T(8,128)S(1)}, f32[2,256,256]{2,1,0:T(8,128)}, u32[]{:S(2)}) copy-start(f32[2,256,256]{2,1,0:T(8,128)} %probe.3) | copy-start | bytes 1572868
  0.7 17.8 %copy-start.2 = (f32[1,1,4,256,256]{4,3,2,1,0:T(8,128)S(1)}, f32[1,1,4,256,256]{4,3,2,1,0:T(8,128)}, u32[]{:S(2)}) copy-start(f32[1,1,4,256,256]{4,3,2,1,0:T(8,128)} %param.12) | copy-start | bytes 3145732
  1.6 1.0 copy-start.14
  18.4 1.0 copy-start.6
  19.5 1.0 copy-start.8
  20.5 1.0 copy-start.10
  21.6 1.0 copy-start.12
  22.6 20.0 %copy-start = (f32[2,512,512]{2,1,0:T(8,128)}, f32[2,512,512]{2,1,0:T(8,128)S(1)}, u32[]{:S(2)}) copy-start(f32[2,512,512]{2,1,0:T(8,128)S(1)} %extend.1.ext.field) | copy-start | bytes 6291460
  42.6 1.3 copy-start.4
  44.0 56.1 %copy-start.7 = (bf16[512,512]{1,0:T(8,128)(2,1)S(1)}, bf16[512,512]{1,0:T(8,128)(2,1)}, u32[]{:S(2)}) copy-start(bf16[512,512]{1,0:T(8,128)(2,1)} %constant.11.clone.bl) | copy-start | bytes 1572868
  44.0 56.1 %copy-start.9 = (bf16[512,512]{1,0:T(8,128)(2,1)S(1)}, bf16[512,512]{1,0:T(8,128)(2,1)}, u32[]{:S(2)}) copy-start(bf16[512,512]{1,0:T(8,128)(2,1)} %constant.10.clone.bh) | copy-start | bytes 1572868
  44.0 56.1 %copy-start.11 = (bf16[512,512]{1,0:T(8,128)(2,1)S(1)}, bf16[512,512]{1,0:T(8,128)(2,1)}, u32[]{:S(2)}) copy-start(bf16[512,512]{1,0:T(8,128)(2,1)} %constant.9.clone.al) | copy-start | bytes 1572868
  44.0 56.1 %copy-start.13 = (bf16[512,512]{1,0:T(8,128)(2,1)S(1)}, bf16[512,512]{1,0:T(8,128)(2,1)}, u32[]{:S(2)}) copy-start(bf16[512,512]{1,0:T(8,128)(2,1)} %constant.8.clone.ah) | copy-start | bytes 1572868
  100.0 20.0 %copy-start.1 = (f32[2,512,512]{2,1,0:T(8,128)}, f32[2,512,512]{2,1,0:T(8,128)S(1)}, u32[]{:S(2)}) copy-start(f32[2,512,512]{2,1,0:T(8,128)S(1)} %get-tuple-element.10.ext.field) | copy-start | bytes 6291460

commit v3 on v2

--- a/solution.py
+++ b/solution.py
@@ -48,13 +48,12 @@
     return cols[:, :width], cols[:, width:]
 
 
-def visit_kernel(offs, ext, probe, coeffs, pats, ah, al, bh, bl, grad, stats, shifted):
+def visit_kernel(offs, ext, probe, coeffs, pats, ah, al, bh, bl, grad, stats):
     width = probe.shape[1]
     size = ext.shape[1]
     tile = size - width
     grad[...] = jnp.zeros_like(grad)
     stats[...] = jnp.zeros_like(stats)
-    shifted[...] = jnp.zeros_like(shifted)
 
     def visit(p, carry):
         oy, ox = offs[p, 0], offs[p, 1]
@@ -89,11 +88,10 @@
         for part, g in ((0, pr * br + pi * bi), (1, pr * bi - pi * br)):
             g = pltpu.roll(jnp.concatenate([g, below], axis=0), odd, axis=0)
             g = pltpu.roll(jnp.concatenate([g, beside], axis=1), ox, axis=1)
-            shifted[part, tile : tile + width + 8, :] = g
-            grad[part] += shifted[part, pl.ds(pl.multiple_of(tile - even, 8), size), :]
+            grad[part, pl.ds(even, width + 8), :] += g
         return carry
 
-    lax.fori_loop(0, pats.shape[0], visit, 0)
+    lax.fori_loop(0, pats.shape[0], visit, 0, unroll=True)
 
 
 def visit_windows(offs, ext, probe, coeffs, pats, stacks):
@@ -108,7 +106,6 @@
         ),
         in_specs=[pl.BlockSpec(memory_space=pltpu.SMEM)] + [vmem] * 8,
         out_specs=(vmem, vmem),
-        scratch_shapes=[pltpu.VMEM((2, 2 * (size - width) + width, size), jnp.float32)],
         compiler_params=pltpu.CompilerParams(vmem_limit_bytes=40 * 1024 * 1024),
         name="visit_windows",
     )(offs, ext, probe, coeffs, pats, *stacks)

time: 162 us -> 151 us (0.932)
  Pallas kernels: 152 us -> 140 us
    pallas_call x2, Pallas kernels: 40 us -> 28.5 us  [visit_windows(): pl.pallas_call(visit_kernel, out_shape=(jax.ShapeDtypeStruct(ext.shape, j...]
where the time goes in v3:
time: 151 us; the launch traced here: 150 us
  Pallas kernels  140 us (93%)
  local copies, waits for them, and re-layouts  9.16 us (6%)
    pallas_call x2, Pallas kernels, update(): pl.pallas_call(functools.partial(update_kernel, last), out_shape=(jax.Sha...  96 us
    pallas_call x2, Pallas kernels, visit_windows(): pl.pallas_call(visit_kernel, out_shape=(jax.ShapeDtypeStruct(ext.shape, j...  28.5 us
    pallas_call x1, Pallas kernels, extend(): pl.pallas_call(functools.partial(extend_kernel, half, tile), out_shape=ja...  15.8 us
    unnamed x32, local copies, waits for them, and re-layouts  8.24 us

profile of v3, /device:TPU:0, one launch (start us, length us, event | category | flops | bytes accessed | tf_op | source)
XLA Modules:
  0.0 150.2 jit_solution(6312183792350247752)
XLA Ops:
  0.6 0.0 copy-start.3
  0.6 0.0 copy-start.5
  0.7 0.0 copy-start.2
  0.7 0.9 copy.12.offs
  1.6 0.0 copy-start.14
  1.6 1.0 copy-done.14
  2.6 15.8 %extend.1.ext.field = f32[2,512,512]{2,1,0:T(8,128)S(1)} custom-call(f32[2,256,256]{2,1,0:T(8,128)S(1)} %copy-done.14), custom_call_target="tpu_custom_call" | custom-call | tf_op jit(solution)/shard_map/extend/pallas_call | solution.py:458
  18.4 0.0 copy-done.3
  18.4 0.0 copy-done.5
  18.4 0.0 copy-done.2
  18.4 0.0 copy-start.6
  18.4 1.0 copy-done.6
  19.5 0.0 copy-start.8
  19.5 1.0 copy-done.8
  20.5 0.0 copy-start.10
  20.5 1.0 copy-done.10
  21.6 0.0 copy-start.12
  21.6 1.0 copy-done.12
  22.6 0.0 copy-start
  22.6 14.4 %visit_windows.2 = (f32[2,512,512]{2,1,0:T(8,128)S(1)}, f32[6,256,256]{2,1,0:T(8,128)S(1)}) custom-call(s32[4,2]{1,0:T(4,128)S(1)} %copy.12.offs, f32[2,512,512]{2,1,0:T(8,128)S(1)} %extend.1.ext.field, f32[2,256,256]{2,1,0:T(8,128)S(1)} %copy-done.5, f32[3,256,256]{2,1,0:T(8,128)S(1)} %copy-done.3, f32[4,256,256]{2,1,0:T(8,128)S(1)} %bitcast.2, ...), custom_call_target="tpu_custom_call" | custom-call | tf_op jit(solution)/shard_map/visit_windows/pallas_call | solution.py:101
  37.1 0.0 copy-done
  37.1 0.0 copy-start.4
  37.1 1.3 copy-done.4
  38.4 0.0 copy-start.7
  38.4 0.0 copy-start.9
  38.4 0.0 copy-start.11
  38.4 0.0 copy-start.13
  38.4 56.0 %update.1 = (f32[2,512,512]{2,1,0:T(8,128)S(1)}, f32[3,256,256]{2,1,0:T(8,128)S(1)}) custom-call(f32[2,512,512]{2,1,0:T(8,128)} %copy-done.4, f32[6,256,256]{2,1,0:T(8,128)S(1)} %get-tuple-element.9.stats, f32[2,512,512]{2,1,0:T(8,128)} %copy-done, f32[3,256,256]{2,1,0:T(8,128)S(1)} %copy-done.3), custom_call_target="tpu_custom_call" | custom-call | tf_op jit(solution)/shard_map/update/pallas_call | solution.py:379
  94.4 0.0 copy-start.1
  94.5 0.0 copy-done.7
  94.5 0.0 copy-done.9
  94.5 0.0 copy-done.11
  94.5 0.0 copy-done.13
  94.5 14.1 %visit_windows.3 = (f32[2,512,512]{2,1,0:T(8,128)S(1)}, f32[6,256,256]{2,1,0:T(8,128)S(1)}) custom-call(s32[4,2]{1,0:T(4,128)S(1)} %copy.12.offs, f32[2,512,512]{2,1,0:T(8,128)S(1)} %get-tuple-element.10.ext.field, f32[2,256,256]{2,1,0:T(8,128)S(1)} %copy-done.5, f32[3,256,256]{2,1,0:T(8,128)S(1)} %get-tuple-element.11.coeffs, f32[4,256,256]{2,1,0:T(8,128)S(1)} %bitcast.3, ...), custom_call_target="tpu_custom_call" | custom-call | tf_op jit(solution)/shard_map/visit_windows/pallas_call | solution.py:101
  108.6 0.0 copy-done.1
  108.6 40.0 %update_last.1 = (f32[2,256,256]{2,1,0:T(8,128)S(1)}, f32[3,256,256]{2,1,0:T(8,128)S(1)}) custom-call(f32[2,512,512]{2,1,0:T(8,128)S(1)} %get-tuple-element.12.grad, f32[6,256,256]{2,1,0:T(8,128)S(1)} %get-tuple-element.13.stats, f32[2,512,512]{2,1,0:T(8,128)} %copy-done.1, f32[3,256,256]{2,1,0:T(8,128)S(1)} %get-tuple-element.11.coeffs), custom_call_target="tpu_custom_call" | custom-call | tf_op jit(solution)/shard_map/update_last/pallas_call | solution.py:379
  148.5 0.8 copy.15
  149.3 0.9 copy.16
Async XLA Ops:
  0.6 17.8 %copy-start.3 = (f32[3,256,256]{2,1,0:T(8,128)S(1)}, f32[3,256,256]{2,1,0:T(8,128)}, u32[]{:S(2)}) copy-start(f32[3,256,256]{2,1,0:T(8,128)} %coeffs.3) | copy-start | bytes 2359300
  0.6 17.8 %copy-start.5 = (f32[2,256,256]{2,1,0:T(8,128)S(1)}, f32[2,256,256]{2,1,0:T(8,128)}, u32[]{:S(2)}) copy-start(f32[2,256,256]{2,1,0:T(8,128)} %probe.3) | copy-start | bytes 1572868
  0.7 17.8 %copy-start.2 = (f32[1,1,4,256,256]{4,3,2,1,0:T(8,128)S(1)}, f32[1,1,4,256,256]{4,3,2,1,0:T(8,128)}, u32[]{:S(2)}) copy-start(f32[1,1,4,256,256]{4,3,2,1,0:T(8,128)} %param.12) | copy-start | bytes 3145732
  1.6 1.0 copy-start.14
  18.4 1.0 copy-start.6
  19.5 1.0 copy-start.8
  20.5 1.0 copy-start.10
  21.6 1.0 copy-start.12
  22.6 14.4 %copy-start = (f32[2,512,512]{2,1,0:T(8,128)}, f32[2,512,512]{2,1,0:T(8,128)S(1)}, u32[]{:S(2)}) copy-start(f32[2,512,512]{2,1,0:T(8,128)S(1)} %extend.1.ext.field) | copy-start | bytes 6291460
  37.1 1.3 copy-start.4
  38.4 56.1 %copy-start.7 = (bf16[512,512]{1,0:T(8,128)(2,1)S(1)}, bf16[512,512]{1,0:T(8,128)(2,1)}, u32[]{:S(2)}) copy-start(bf16[512,512]{1,0:T(8,128)(2,1)} %constant.11.clone.bl) | copy-start | bytes 1572868
  38.4 56.1 %copy-start.9 = (bf16[512,512]{1,0:T(8,128)(2,1)S(1)}, bf16[512,512]{1,0:T(8,128)(2,1)}, u32[]{:S(2)}) copy-start(bf16[512,512]{1,0:T(8,128)(2,1)} %constant.10.clone.bh) | copy-start | bytes 1572868
  38.4 56.1 %copy-start.11 = (bf16[512,512]{1,0:T(8,128)(2,1)S(1)}, bf16[512,512]{1,0:T(8,128)(2,1)}, u32[]{:S(2)}) copy-start(bf16[512,512]{1,0:T(8,128)(2,1)} %constant.9.clone.al) | copy-start | bytes 1572868
  38.4 56.1 %copy-start.13 = (bf16[512,512]{1,0:T(8,128)(2,1)S(1)}, bf16[512,512]{1,0:T(8,128)(2,1)}, u32[]{:S(2)}) copy-start(bf16[512,512]{1,0:T(8,128)(2,1)} %constant.8.clone.ah) | copy-start | bytes 1572868
  94.4 14.1 %copy-start.1 = (f32[2,512,512]{2,1,0:T(8,128)}, f32[2,512,512]{2,1,0:T(8,128)S(1)}, u32[]{:S(2)}) copy-start(f32[2,512,512]{2,1,0:T(8,128)S(1)} %get-tuple-element.10.ext.field) | copy-start | bytes 6291460
